TPU v7x, 256 devices: a whole 4x4x8 slice. The times are simulated.
256 devices in a mesh: list: 64 (over z_lo, y, x, core), row: 4 (over z_hi).
Axes of the slice: x: 4, y: 4, z: 8 (z_hi: 4, z_lo: 2; z = z_hi * 2 + z_lo), core: 2. Of those that a mesh axis runs over, the one named last changes fastest.
Arguments:
- corpus: bfloat16 [262144, 768], P(('list', 'row')), may hold values from -6 to 6
- row_list: int32 [262144], P(('list', 'row')), may hold values from 0 to 4095, as said below
- list_slot: int32 [4096], replicated, may hold values from 0 to 4095, as said below
- member_counts: int32 [4096], P('list'), may hold values from 32 to 96, as said below
- old_centroids: float32 [4096, 768], P('list'), may hold values from -6 to 6
- next_rows: bfloat16 [393216, 768], P(('list', 'row')), may hold values from -6 to 6
Outputs:
- new_centroids: float32 [4096, 768], P('list')
- best_score: float32 [393216], P(('list', 'row'))
Inputs may be any that keep to these rules, and one draw needn't show every extreme that they name: `row_list`: each device sends every owner (list_slot // 64) at least 8 and at most 24 of its rows; some owner receives 24 rows from every device. `list_slot`: A permutation of the list numbers. `member_counts`: the exact number of corpus rows in each slot's list; the lists of one owner differ by at most one.
All inputs are finite; a program needn't handle non-finite values.
Results may differ from a plain program's by a relative error of at most 0.0025.
Values may be sent and summed in bfloat16 or wider, within the bound.
A program may use at most 64 MiB of HBM per device.

v0:
```python
import jax
import jax.numpy as jnp
from jax import lax
from jax.sharding import PartitionSpec as P

ITERS = 3
eps_norm = 1e-06
aniso_par = 32.0
perp_weight = 1.0
prior_weight = 16.0


def unit_of(row_block):
    values = row_block.astype(jnp.float32)
    scaled = values / jnp.sqrt(jnp.sum(values * values, axis=1, keepdims=True) + eps_norm)
    return scaled.astype(jnp.bfloat16)


def split_pair(values):
    high_part = values.astype(jnp.bfloat16)
    low_part = (values - high_part.astype(jnp.float32)).astype(jnp.bfloat16)
    return (high_part, low_part)


def prepare(member_block, member_local, lists_own):
    unit_rows = unit_of(member_block)
    membership = (member_local[:, None] == jnp.arange(lists_own, dtype=jnp.int32)[None, :]).astype(
        jnp.float32
    )
    return (unit_rows, membership)


def gram_part(unit_rows, membership, vectors):
    inner_dims = (((1,), (1,)), ((), ()))
    outer_dims = (((0,), (0,)), ((), ()))
    vec_high, vec_low = split_pair(vectors)
    scores = lax.dot_general(unit_rows, vec_high, inner_dims, preferred_element_type=jnp.float32)
    scores = scores + lax.dot_general(
        unit_rows, vec_low, inner_dims, preferred_element_type=jnp.float32
    )
    weighted = scores * membership
    wgt_high, wgt_low = split_pair(weighted)
    result = lax.dot_general(wgt_high, unit_rows, outer_dims, preferred_element_type=jnp.float32)
    return result + lax.dot_general(
        wgt_low, unit_rows, outer_dims, preferred_element_type=jnp.float32
    )


def member_total(membership, member_block):
    return lax.dot_general(
        membership.astype(jnp.bfloat16),
        member_block,
        (((0,), (0,)), ((), ())),
        preferred_element_type=jnp.float32,
    )


def on_device(corpus, row_list, list_slot, member_counts, old_centroids, next_rows):
    n_owner = lax.axis_size("list")
    lists_own = old_centroids.shape[0]
    local_rows = corpus.shape[0]
    cap_slots = 3 * local_rows // (2 * n_owner)
    width = corpus.shape[1]
    slot_ids = jnp.take(list_slot, row_list)
    owner_id = slot_ids // lists_own
    local_id = slot_ids % lists_own
    hits = (owner_id[:, None] == jnp.arange(n_owner, dtype=jnp.int32)[None, :]).astype(jnp.int32)
    rank_in = jnp.sum((jnp.cumsum(hits, axis=0) - 1) * hits, axis=1)
    dest_idx = owner_id * cap_slots + rank_in
    send_rows = (
        jnp.zeros((n_owner * cap_slots, width), jnp.bfloat16)
        .at[dest_idx]
        .set(corpus)
        .reshape(n_owner, cap_slots, width)
    )
    send_local = (
        jnp.full((n_owner * cap_slots,), -1, jnp.int32)
        .at[dest_idx]
        .set(local_id)
        .reshape(n_owner, cap_slots)
    )
    recv_rows, recv_local = (
        lax.all_to_all(send_rows, "list", split_axis=0, concat_axis=0, tiled=True),
        lax.all_to_all(send_local, "list", split_axis=0, concat_axis=0, tiled=True),
    )
    recv_rows = recv_rows.reshape(n_owner * cap_slots, width)
    recv_local = recv_local.reshape(n_owner * cap_slots)
    centroids = old_centroids
    unit_rows, membership = prepare(recv_rows, recv_local, lists_own)
    row_sums, first_gram = lax.psum(
        (member_total(membership, recv_rows), gram_part(unit_rows, membership, centroids)), "row"
    )
    diag_term = perp_weight * member_counts.astype(jnp.float32)[:, None] + prior_weight
    residual = (
        aniso_par * row_sums
        + prior_weight * centroids
        - (diag_term * centroids + (aniso_par - perp_weight) * first_gram)
    )
    direction = residual
    norm_now = jnp.sum(residual * residual, axis=1, keepdims=True)
    for iteration in range(ITERS):
        applied = diag_term * direction + (aniso_par - perp_weight) * lax.psum(
            gram_part(unit_rows, membership, direction), "row"
        )
        step_len = norm_now / jnp.sum(direction * applied, axis=1, keepdims=True)
        centroids = centroids + step_len * direction
        residual = residual - step_len * applied
        norm_next = jnp.sum(residual * residual, axis=1, keepdims=True)
        direction = residual + norm_next / norm_now * direction
        norm_now = norm_next
    panel = centroids.astype(jnp.bfloat16)
    start_score = jnp.full((next_rows.shape[0],), -jnp.inf, jnp.float32)
    piece = lax.all_gather(panel, "list", axis=0, tiled=True)
    piece_rows = piece.shape[0]
    block_size = 512
    blocks = piece.reshape(piece_rows // block_size, block_size, piece.shape[1])

    def one_block(running, piece_block):
        scores = lax.dot_general(
            next_rows, piece_block, (((1,), (1,)), ((), ())), preferred_element_type=jnp.float32
        )
        return (jnp.maximum(running, jnp.max(scores, axis=1)), None)

    result, unused = lax.scan(one_block, start_score, blocks)
    return (centroids, result / width)


def solution(mesh):
    in_specs = (
        P(("list", "row"), None),
        P(("list", "row")),
        P(),
        P("list"),
        P("list", None),
        P(("list", "row"), None),
    )
    out_specs = (P("list", None), P(("list", "row")))
    return jax.shard_map(
        on_device, mesh=mesh, in_specs=in_specs, out_specs=out_specs, check_vma=False
    )
```

profile of v0, /device:TPU:1, one launch (start us, length us, event | category | flops | bytes accessed | tf_op | source)
XLA Modules:
  0.0 470.4 jit_solution(17790374509922220616)
XLA Ops:
  7.9 6.1 %gather_fusion = s32[1024]{0:T(1024)S(1)} fusion(s32[4096]{0:T(1024)S(1)} %copy-done, s32[1024]{0:T(1024)S(1)} %fusion.41), kind=kCustom, calls=%fused_computation | custom fusion | bytes 12288 | tf_op jit(solution)/shard_map/jit(_take)/gather | solution.py:64
  14.2 18.0 %reduce-window.6 = s32[64,8,128]{2,1,0:T(8,128)S(1)} reduce-window(s32[64,8,128]{2,1,0:T(8,128)S(1)} %fusion.11, s32[]{:T(128)} %constant.69.clone.1), window={size=1x1x128 pad=0_0x0_0x127_0}, to_apply=%region_0.1 | reduce-window | flops 8323072 | bytes 524292 | tf_op jit(solution)/shard_map/reduce-window
  32.8 4.3 scatter_custom_fusion
  37.8 10.3 %all-to-all-start = ((s32[64,1,24]{2,1,0:T(1,128)}), s32[64,1,24]{2,1,0:T(1,128)S(1)}, u32[]{:S(2)}, u32[]{:S(2)}) async-start(s32[64,1,24]{2,1,0:T(1,128)} %bitcast.3), calls=%async_computation | async-start | bytes 65536 | tf_op jit(solution)/shard_map/all_to_all | solution.py:84
  48.2 7.5 %scatter_custom_fusion.1 = bf16[1536,768]{1,0:T(8,128)(2,1)} fusion(s32[1024]{0:T(1024)S(1)} %compare_select_fusion, bf16[1024,768]{1,0:T(8,128)(2,1)} %param.8, bf16[]{:T(256)} %constant.79.clone.1), kind=kCustom, calls=%fused_computation.18 | custom fusion | bytes 2359808 | tf_op jit(solution)/shard_map/scatter | solution.py:73
  55.9 8.6 %all-to-all-start.1 = ((bf16[64,24,768]{2,1,0:T(8,128)(2,1)}), bf16[64,24,768]{2,1,0:T(8,128)(2,1)S(1)}, u32[]{:S(2)}, u32[]{:S(2)}) async-start(bf16[64,24,768]{2,1,0:T(8,128)(2,1)} %bitcast.46), calls=%async_computation.1 | async-start | bytes 4718592 | tf_op jit(solution)/shard_map/all_to_all | solution.py:83
  65.9 29.0 %all-to-all-done.1 = bf16[64,24,768]{2,1,0:T(8,128)(2,1)S(1)} async-done(((bf16[64,24,768]{2,1,0:T(8,128)(2,1)}), bf16[64,24,768]{2,1,0:T(8,128)(2,1)S(1)}, u32[]{:S(2)}, u32[]{:S(2)}) %all-to-all-start.1) | async-done | bytes 2359328 | tf_op jit(solution)/shard_map/all_to_all | solution.py:83
  96.5 2.2 divide_convert_fusion
  100.9 1.2 convolution_add_fusion.7
  102.1 1.2 fusion.12
  103.6 52.9 %all-reduce.12.cloned.1.call-done = (f32[64,768]{1,0:T(8,128)}, f32[64,768]{1,0:T(8,128)}) async-done(((f32[64,768]{1,0:T(8,128)}, f32[64,768]{1,0:T(8,128)}), (f32[64,768]{1,0:T(8,128)}, f32[64,768]{1,0:T(8,128)})) %all-reduce.12.cloned.1.call-update) | async-done | bytes 393232 | tf_op jit(solution)/shard_map/psum | solution.py:90
  159.7 1.2 convolution_add_fusion.6
  161.0 49.5 %all-reduce.6.cloned.1.call-done = f32[64,768]{1,0:T(8,128)} async-done(((f32[64,768]{1,0:T(8,128)}), f32[64,768]{1,0:T(8,128)}) %all-reduce.6.cloned.1.call-update) | async-done | bytes 196624 | tf_op jit(solution)/shard_map/psum | solution.py:102
  210.5 1.1 multiply_reduce_fusion.5
  211.7 1.1 multiply_reduce_fusion.4
  215.1 1.2 convolution_add_fusion.5
  216.4 49.2 %all-reduce.8.cloned.1.call-done = f32[64,768]{1,0:T(8,128)} async-done(((f32[64,768]{1,0:T(8,128)}), f32[64,768]{1,0:T(8,128)}) %all-reduce.8.cloned.1.call-update) | async-done | bytes 196624 | tf_op jit(solution)/shard_map/psum | solution.py:102
  265.6 1.1 multiply_reduce_fusion.3
  266.8 1.1 multiply_reduce_fusion.2
  271.2 1.2 convolution_add_fusion.4
  272.5 49.3 %all-reduce.10.cloned.1.call-done = f32[64,768]{1,0:T(8,128)} async-done(((f32[64,768]{1,0:T(8,128)}), f32[64,768]{1,0:T(8,128)}) %all-reduce.10.cloned.1.call-update) | async-done | bytes 196624 | tf_op jit(solution)/shard_map/psum | solution.py:102
  321.8 1.1 multiply_reduce_fusion.1
  323.7 112.5 %all-gather.2.cloned.1.call-done = bf16[4096,768]{1,0:T(8,128)(2,1)} async-done(((bf16[64,768]{1,0:T(8,128)(2,1)}), bf16[4096,768]{1,0:T(8,128)(2,1)}) %all-gather.2.cloned.1.call-update) | async-done | bytes 6291472 | tf_op jit(solution)/shard_map/all_gather | solution.py:113
  436.2 27.1 %while.11 = (s32[]{:T(128)}, f32[1536]{0:T(1024)S(1)}, bf16[8,512,768]{2,1,0:T(8,128)(2,1)}, bf16[1536,768]{1,0:T(8,128)(2,1)}, s32[]{:T(128)}, /*index=5*/s32[]{:T(128)}) while((s32[]{:T(128)}, f32[1536]{0:T(1024)S(1)}, bf16[8,512,768]{2,1,0:T(8,128)(2,1)}, bf16[1536,768]{1,0:T(8,128)(2,1)}, s32[]{:T(128)}, ...), condition=%wide.region_19.20_spmd.clone, body=%wide.region_17.19_spmd.clone.sunk | while | flops 1208747520 | bytes 3170895 | solution.py:124
  436.2 3.3 convolution_reduce_fusion.2
  439.6 3.3 convolution_reduce_fusion.2
  443.0 3.3 convolution_reduce_fusion.2
  446.4 3.3 convolution_reduce_fusion.2
  449.8 3.3 convolution_reduce_fusion.2
  453.2 3.3 convolution_reduce_fusion.2
  456.5 3.3 convolution_reduce_fusion.2
  459.9 3.3 convolution_reduce_fusion.2
  (73 shorter events, 18.1 us)
Async XLA Ops:
  7.2 0.8 copy-start
  7.2 6.9 %copy-start.4 = (s32[1024]{0:T(1024)S(1)}, s32[1024]{0:T(1024)}, u32[]{:S(2)}) copy-start(s32[1024]{0:T(1024)} %param.9) | copy-start | bytes 12292
  37.8 18.1 %all-to-all-start = ((s32[64,1,24]{2,1,0:T(1,128)}), s32[64,1,24]{2,1,0:T(1,128)S(1)}, u32[]{:S(2)}, u32[]{:S(2)}) async-start(s32[64,1,24]{2,1,0:T(1,128)} %bitcast.3), calls=%async_computation | async-start | bytes 65536 | tf_op jit(solution)/shard_map/all_to_all | solution.py:84
  55.9 39.0 %all-to-all-start.1 = ((bf16[64,24,768]{2,1,0:T(8,128)(2,1)}), bf16[64,24,768]{2,1,0:T(8,128)(2,1)S(1)}, u32[]{:S(2)}, u32[]{:S(2)}) async-start(bf16[64,24,768]{2,1,0:T(8,128)(2,1)} %bitcast.46), calls=%async_computation.1 | async-start | bytes 4718592 | tf_op jit(solution)/shard_map/all_to_all | solution.py:83
  64.6 91.9 %all-reduce.12.cloned.1.call-start = ((), (), s32[]{:S(2)}) async-start(), calls=%async_computation.6 | async-start | bytes 786432 | tf_op jit(solution)/shard_map/psum | solution.py:90
  95.0 1.4 copy-start.1
  96.5 2.2 copy-start.3
  100.4 1.7 copy-start.2
  100.9 2.7 copy-start.5
  103.3 107.2 %all-reduce.6.cloned.1.call-start = ((), (), s32[]{:S(2)}) async-start(), calls=%async_computation.2 | async-start | bytes 393216 | tf_op jit(solution)/shard_map/psum | solution.py:102
  161.0 104.7 %all-reduce.8.cloned.1.call-start = ((), (), s32[]{:S(2)}) async-start(), calls=%async_computation.3 | async-start | bytes 393216 | tf_op jit(solution)/shard_map/psum | solution.py:102
  216.3 105.4 %all-reduce.10.cloned.1.call-start = ((), (), s32[]{:S(2)}) async-start(), calls=%async_computation.4 | async-start | bytes 393216 | tf_op jit(solution)/shard_map/psum | solution.py:102
  272.4 163.8 %all-gather.2.cloned.1.call-start = ((), (), s32[]{:S(2)}) async-start(), calls=%async_computation.5 | async-start | bytes 6389760 | tf_op jit(solution)/shard_map/all_gather | solution.py:113
Sparse Core Ops, SparseCore 0:
  103.5 52.9 all-reduce.11
  161.1 49.3 all-reduce.5
  216.5 49.1 all-reduce.7
  272.5 49.1 all-reduce.9
  323.9 112.3 all-gather.1
where the time goes:
time: 471 us; the launch traced here: 470 us
  waiting for transfers between devices  343 us (73%)
  matrix products  41.5 us (9%)
  other arithmetic  31.9 us (7%)
  local copies, waits for them, and re-layouts  20.6 us (4%)
  starting transfers between devices  19.3 us (4%)
  between operations  14.1 us (3%)
    psum x3, waiting for transfers between devices, on_device(): lax.psum(gram_part(unit_rows, membership, direction), 'row')  148 us
    all_gather x1, waiting for transfers between devices, on_device(): piece = lax.all_gather(panel, 'list', axis=0, tiled=True)  112 us
    psum x1, waiting for transfers between devices, on_device(): lax.psum((member_total(membership, recv_rows), gram_part(unit_rows, membe...  52.9 us
    all_to_all x1, waiting for transfers between devices, on_device(): lax.all_to_all(send_rows, 'list', split_axis=0, concat_axis=0, tiled=True)  29 us
    dot_general x8, matrix products, one_block(): lax.dot_general(next_rows, piece_block, (((1,), (1,)), ((), ())), preferr...  26.8 us
    another operation x2, other arithmetic  18 us
    all_to_all x1, starting transfers between devices, on_device(): lax.all_to_all(send_local, 'list', split_axis=0, concat_axis=0, tiled=True)  10.3 us
  transfers between devices with their start and end apart: 7, of which 7 were waited for; matrix products, arithmetic and copies ran while one was open for 2% of the time, Pallas kernels for 0%

commit v1 on v0

--- a/solution.py
+++ b/solution.py
@@ -8,6 +8,12 @@
 aniso_par = 32.0
 perp_weight = 1.0
 prior_weight = 16.0
+
+
+def summed_here(array, axis):
+    parts = lax.all_gather(array, axis, axis=0, tiled=False)
+    summed = parts.sum(axis=0)
+    return summed
 
 
 def unit_of(row_block):
@@ -99,7 +105,7 @@
     direction = residual
     norm_now = jnp.sum(residual * residual, axis=1, keepdims=True)
     for iteration in range(ITERS):
-        applied = diag_term * direction + (aniso_par - perp_weight) * lax.psum(
+        applied = diag_term * direction + (aniso_par - perp_weight) * summed_here(
             gram_part(unit_rows, membership, direction), "row"
         )
         step_len = norm_now / jnp.sum(direction * applied, axis=1, keepdims=True)

time: 471 us -> 378 us (0.80)
  waiting for transfers between devices: 343 us -> 199 us
  blocking collectives: 0 us -> 51.7 us
    psum x3 -> x0, waiting for transfers between devices: 148 us -> none  [on_device(): lax.psum(gram_part(unit_rows, membership, direction), 'row')]
    all_gather x0 -> x3, blocking collectives: none -> 51.7 us  [summed_here(): parts = lax.all_gather(array, axis, axis=0, tiled=False)]
  transfers between devices with their start and end apart: 7 -> 4, of which waited for: 7 -> 4; matrix products, arithmetic and copies ran while one was open for 2% -> 2% of each run, Pallas kernels for 0% -> 0%
where the time goes in v1:
time: 378 us; the launch traced here: 377 us
  waiting for transfers between devices  199 us (53%)
  blocking collectives  51.7 us (14%)
  matrix products  39.4 us (10%)
  other arithmetic  31.5 us (8%)
  local copies, waits for them, and re-layouts  21.6 us (6%)
  starting transfers between devices  19.2 us (5%)
  between operations  14.5 us (4%)
    all_gather x1, waiting for transfers between devices, on_device(): piece = lax.all_gather(panel, 'list', axis=0, tiled=True)  117 us
    psum x1, waiting for transfers between devices, on_device(): lax.psum((member_total(membership, recv_rows), gram_part(unit_rows, membe...  52.9 us
    all_gather x3, blocking collectives, summed_here(): parts = lax.all_gather(array, axis, axis=0, tiled=False)  51.7 us
    all_to_all x1, waiting for transfers between devices, on_device(): lax.all_to_all(send_rows, 'list', split_axis=0, concat_axis=0, tiled=True)  29 us
    dot_general x8, matrix products, one_block(): lax.dot_general(next_rows, piece_block, (((1,), (1,)), ((), ())), preferr...  26.8 us
    another operation x2, other arithmetic  18 us
    all_to_all x1, starting transfers between devices, on_device(): lax.all_to_all(send_local, 'list', split_axis=0, concat_axis=0, tiled=True)  10.3 us
    all_to_all x1, starting transfers between devices, on_device(): lax.all_to_all(send_rows, 'list', split_axis=0, concat_axis=0, tiled=True)  8.61 us
  transfers between devices with their start and end apart: 4, of which 4 were waited for; matrix products, arithmetic and copies ran while one was open for 2% of the time, Pallas kernels for 0%

profile of v1, /device:TPU:1, one launch (start us, length us, event | category | flops | bytes accessed | tf_op | source)
XLA Modules:
  0.0 377.1 jit_solution(3369705497837245185)
XLA Ops:
  7.9 6.1 %gather_fusion = s32[1024]{0:T(1024)S(1)} fusion(s32[4096]{0:T(1024)S(1)} %copy-done, s32[1024]{0:T(1024)S(1)} %fusion.41), kind=kCustom, calls=%fused_computation | custom fusion | bytes 12288 | tf_op jit(solution)/shard_map/jit(_take)/gather | solution.py:70
  14.2 18.0 %reduce-window.6 = s32[64,8,128]{2,1,0:T(8,128)S(1)} reduce-window(s32[64,8,128]{2,1,0:T(8,128)S(1)} %fusion.11, s32[]{:T(128)} %constant.69.clone.1), window={size=1x1x128 pad=0_0x0_0x127_0}, to_apply=%region_0.1 | reduce-window | flops 8323072 | bytes 524292 | tf_op jit(solution)/shard_map/reduce-window
  32.8 4.3 %scatter_custom_fusion = s32[1536]{0:T(1024)S(1)} fusion(s32[1024]{0:T(1024)S(1)} %compare_select_fusion, s32[1024]{0:T(1024)S(1)} %get-tuple-element.56, s32[]{:T(128)} %constant.68.clone.1), kind=kCustom, calls=%fused_computation.91 | custom fusion | bytes 6148 | tf_op jit(solution)/shard_map/scatter | solution.py:85
  37.8 10.3 %all-to-all-start = ((s32[64,1,24]{2,1,0:T(1,128)}), s32[64,1,24]{2,1,0:T(1,128)S(1)}, u32[]{:S(2)}, u32[]{:S(2)}) async-start(s32[64,1,24]{2,1,0:T(1,128)} %bitcast.3), calls=%async_computation | async-start | bytes 65536 | tf_op jit(solution)/shard_map/all_to_all | solution.py:90
  48.2 7.5 %scatter_custom_fusion.1 = bf16[1536,768]{1,0:T(8,128)(2,1)} fusion(s32[1024]{0:T(1024)S(1)} %compare_select_fusion, bf16[1024,768]{1,0:T(8,128)(2,1)} %param.8, bf16[]{:T(256)} %constant.79.clone.1), kind=kCustom, calls=%fused_computation.18 | custom fusion | bytes 2359808 | tf_op jit(solution)/shard_map/scatter | solution.py:79
  55.9 8.6 %all-to-all-start.1 = ((bf16[64,24,768]{2,1,0:T(8,128)(2,1)}), bf16[64,24,768]{2,1,0:T(8,128)(2,1)S(1)}, u32[]{:S(2)}, u32[]{:S(2)}) async-start(bf16[64,24,768]{2,1,0:T(8,128)(2,1)} %bitcast.49), calls=%async_computation.1 | async-start | bytes 4718592 | tf_op jit(solution)/shard_map/all_to_all | solution.py:89
  66.0 29.0 %all-to-all-done.1 = bf16[64,24,768]{2,1,0:T(8,128)(2,1)S(1)} async-done(((bf16[64,24,768]{2,1,0:T(8,128)(2,1)}), bf16[64,24,768]{2,1,0:T(8,128)(2,1)S(1)}, u32[]{:S(2)}, u32[]{:S(2)}) %all-to-all-start.1) | async-done | bytes 2359328 | tf_op jit(solution)/shard_map/all_to_all | solution.py:89
  95.5 0.9 copy-done.1
  96.5 2.2 divide_convert_fusion
  99.5 0.8 fusion.6
  100.9 1.2 convolution_add_fusion.7
  102.1 1.2 fusion.12
  103.6 52.9 %all-reduce.3.cloned.1.call-done = (f32[64,768]{1,0:T(8,128)}, f32[64,768]{1,0:T(8,128)}) async-done(((f32[64,768]{1,0:T(8,128)}, f32[64,768]{1,0:T(8,128)}), (f32[64,768]{1,0:T(8,128)}, f32[64,768]{1,0:T(8,128)})) %all-reduce.3.cloned.1.call-update) | async-done | bytes 393232 | tf_op jit(solution)/shard_map/psum | solution.py:96
  156.4 1.1 add_subtract_fusion
  160.3 16.9 %all-gather = f32[256,768]{1,0:T(8,128)S(1)} all-gather(f32[64,768]{1,0:T(8,128)S(1)} %convolution_add_fusion.6), channel_id=2, replica_groups=mesh['list'=64,'row'=4] {'row'}, dimensions={0}, use_global_device_ids=true | all-gather | bytes 983040 | tf_op jit(solution)/shard_map/all_gather | solution.py:14
  177.9 1.1 multiply_reduce_fusion.5
  179.1 1.1 multiply_reduce_fusion.4
  181.7 0.8 fusion.4
  183.6 18.2 %all-gather.1 = f32[256,768]{1,0:T(8,128)} all-gather(f32[64,768]{1,0:T(8,128)S(1)} %convolution_add_fusion.5), channel_id=3, replica_groups=mesh['list'=64,'row'=4] {'row'}, dimensions={0}, use_global_device_ids=true | all-gather | bytes 983040 | tf_op jit(solution)/shard_map/all_gather | solution.py:14
  201.8 1.2 reduce_sum.105
  203.0 0.9 multiply_reduce_fusion.3
  208.2 16.6 %all-gather.2 = f32[256,768]{1,0:T(8,128)S(1)} all-gather(f32[64,768]{1,0:T(8,128)S(1)} %convolution_add_fusion.4), channel_id=4, replica_groups=mesh['list'=64,'row'=4] {'row'}, dimensions={0}, use_global_device_ids=true | all-gather | bytes 983040 | tf_op jit(solution)/shard_map/all_gather | solution.py:14
  225.9 116.8 %all-gather.5.cloned.1.call-done = bf16[4096,768]{1,0:T(8,128)(2,1)} async-done(((bf16[64,768]{1,0:T(8,128)(2,1)}), bf16[4096,768]{1,0:T(8,128)(2,1)}) %all-gather.5.cloned.1.call-update) | async-done | bytes 6291472 | tf_op jit(solution)/shard_map/all_gather | solution.py:119
  342.6 27.1 %while.11 = (s32[]{:T(128)}, f32[1536]{0:T(1024)S(1)}, bf16[8,512,768]{2,1,0:T(8,128)(2,1)}, bf16[1536,768]{1,0:T(8,128)(2,1)}, s32[]{:T(128)}, /*index=5*/s32[]{:T(128)}) while((s32[]{:T(128)}, f32[1536]{0:T(1024)S(1)}, bf16[8,512,768]{2,1,0:T(8,128)(2,1)}, bf16[1536,768]{1,0:T(8,128)(2,1)}, s32[]{:T(128)}, ...), condition=%wide.region_19.20_spmd.clone, body=%wide.region_17.19_spmd.clone.sunk | while | flops 1208747520 | bytes 3170895 | solution.py:130
  342.6 3.3 convolution_reduce_fusion.2
  346.0 3.3 convolution_reduce_fusion.2
  349.4 3.3 convolution_reduce_fusion.2
  352.8 3.3 convolution_reduce_fusion.2
  356.1 3.3 convolution_reduce_fusion.2
  359.5 3.3 convolution_reduce_fusion.2
  362.9 3.3 convolution_reduce_fusion.2
  366.3 3.3 convolution_reduce_fusion.2
  (98 shorter events, 17.8 us)
Async XLA Ops:
  7.2 0.8 copy-start
  7.2 6.9 %copy-start.10 = (s32[1024]{0:T(1024)S(1)}, s32[1024]{0:T(1024)}, u32[]{:S(2)}) copy-start(s32[1024]{0:T(1024)} %param.9) | copy-start | bytes 12292
  37.8 18.1 %all-to-all-start = ((s32[64,1,24]{2,1,0:T(1,128)}), s32[64,1,24]{2,1,0:T(1,128)S(1)}, u32[]{:S(2)}, u32[]{:S(2)}) async-start(s32[64,1,24]{2,1,0:T(1,128)} %bitcast.3), calls=%async_computation | async-start | bytes 65536 | tf_op jit(solution)/shard_map/all_to_all | solution.py:90
  55.9 39.0 %all-to-all-start.1 = ((bf16[64,24,768]{2,1,0:T(8,128)(2,1)}), bf16[64,24,768]{2,1,0:T(8,128)(2,1)S(1)}, u32[]{:S(2)}, u32[]{:S(2)}) async-start(bf16[64,24,768]{2,1,0:T(8,128)(2,1)} %bitcast.49), calls=%async_computation.1 | async-start | bytes 4718592 | tf_op jit(solution)/shard_map/all_to_all | solution.py:89
  64.6 91.9 %all-reduce.3.cloned.1.call-start = ((), (), s32[]{:S(2)}) async-start(), calls=%async_computation.3 | async-start | bytes 786432 | tf_op jit(solution)/shard_map/psum | solution.py:96
  65.9 92.4 %copy-start.4 = (s32[1536]{0:T(1024)}, s32[1536]{0:T(1024)S(1)}, u32[]{:S(2)}) copy-start(s32[1536]{0:T(1024)S(1)} %eq.47) | copy-start | bytes 18436
  95.0 1.4 copy-start.1
  96.5 2.2 copy-start.3
  100.4 1.7 copy-start.2
  100.9 2.7 copy-start.19
  103.3 239.3 %all-gather.5.cloned.1.call-start = ((), (), s32[]{:S(2)}) async-start(), calls=%async_computation.2 | async-start | bytes 6389760 | tf_op jit(solution)/shard_map/all_gather | solution.py:119
  103.6 55.6 %copy-start.7 = (f32[64]{0:T(128)}, f32[64]{0:T(128)S(1)}, u32[]{:S(2)}) copy-start(f32[64]{0:T(128)S(1)} %convert_add_fusion) | copy-start | bytes 772
  177.9 3.8 copy-start.5
  179.1 1.2 copy-start.13
  180.2 0.5 copy-start.17
  183.6 20.3 %copy-start.18 = (f32[64]{0:T(128)S(1)}, f32[64]{0:T(128)}, u32[]{:S(2)}) copy-start(f32[64]{0:T(128)} %copy-done.17) | copy-start | bytes 772
  183.6 20.3 %copy-start.8 = (f32[64]{0:T(128)S(1)}, f32[64]{0:T(128)}, u32[]{:S(2)}) copy-start(f32[64]{0:T(128)} %copy-done.7) | copy-start | bytes 772
  203.0 3.3 copy-start.6
  203.9 0.7 copy-start.11
  204.1 0.5 copy-start.15
  207.6 17.2 %copy-start.9 = (f32[64]{0:T(128)S(1)}, f32[64]{0:T(128)}, u32[]{:S(2)}) copy-start(f32[64]{0:T(128)} %copy-done.7) | copy-start | bytes 772
  207.6 17.4 %copy-start.16 = (f32[64]{0:T(128)S(1)}, f32[64]{0:T(128)}, u32[]{:S(2)}) copy-start(f32[64]{0:T(128)} %copy-done.15) | copy-start | bytes 772
  207.6 17.4 %copy-start.12 = (f32[64]{0:T(128)S(1)}, f32[64]{0:T(128)}, u32[]{:S(2)}) copy-start(f32[64]{0:T(128)} %copy-done.11) | copy-start | bytes 772
  207.6 17.4 %copy-start.14 = (f32[64]{0:T(128)S(1)}, f32[64]{0:T(128)}, u32[]{:S(2)}) copy-start(f32[64]{0:T(128)} %copy-done.13) | copy-start | bytes 772
Sparse Core Ops, SparseCore 0:
  103.5 52.9 all-reduce.2
  226.0 116.5 all-gather.4
